TPU v7x, 32 devices: a whole 2x2x4 slice. The times are simulated.
32 devices in a mesh: leaf: 32 (over z, y, x, core).
Axes of the slice: x: 2, y: 2, z: 4, core: 2. Of those that a mesh axis runs over, the one named last changes fastest.
Arguments:
- points: bfloat16 [64, 131072], P(None, 'leaf'), may hold values from -5 to 5
- charges: bfloat16 [32, 131072], P(None, 'leaf'), may hold values from -1.5 to 1.5
- leaf_order: int32 [32, 4096], P('leaf'), may hold values from 0 to 4095, each once within a row
- near_list: int32 [512, 16], P('leaf'), may hold values from -1 to 511, as said below
- far_list: int32 [256, 8], P('leaf'), may hold values from -1 to 7
- local_skel: int32 [480, 256], P('leaf'), may hold values from 0 to 511, as said below
- upper_skel: int32 [30, 256], replicated, may hold values from 0 to 511, as said below
Outputs:
- potentials: float32 [32, 131072], P(None, 'leaf')
- root_field: float32 [32, 32, 256], P('leaf')
Inputs may be any that keep to these rules, and one draw needn't show every extreme that they name: `leaf_order`: each row is a permutation of the positions of one device's points. `near_list`: slot 0 of leaf g's row is g itself; every other entry is -1 or a leaf h different from g with |h - g| <= 16, and the leaves of one row are distinct. `far_list`: an entry other than -1 names a level-one node of the same device subtree, counted from that subtree's first level-one node; entries of a row may repeat. `local_skel`: the entries of a row are distinct. `upper_skel`: the entries of a row are distinct.
All inputs are finite; a program needn't handle non-finite values.
Results may differ from a plain program's by a relative error of at most 0.0014.
Values may be sent and summed in bfloat16 or wider, within the bound.
No kernel may reach another device: no remote copies, remote signals or barrier semaphores. Data moves between devices by JAX's collectives and lax.ppermute only.
A program may use at most 64 MiB of HBM per device.

v0:
```python
import functools
import math

import jax
import jax.numpy as jnp
from jax import lax
from jax.experimental import pallas as pl
from jax.experimental.pallas import tpu as pltpu
from jax.sharding import PartitionSpec as P

PAIR_GAIN = math.sqrt(2.0)
LOG2E = math.log2(math.e)
BF = jnp.bfloat16
F32 = jnp.float32
NT = (((1,), (1,)), ((), ()))
AUX = 8
PARTS = (0.25, 0.125)
ROW, BLOCK = 36, 12
OWN_ROWS = (2, 2)
ANY_ROWS = (1, 1, 1)
UNROLL = 4
VMEM = pl.BlockSpec(memory_space=pltpu.VMEM)
SMEM = pl.BlockSpec(memory_space=pltpu.SMEM)
HBM = pl.BlockSpec(memory_space=pltpu.HBM)
ANY = pl.BlockSpec(memory_space=pl.ANY)


def nt_dot(a, b):
    return lax.dot_general(a, b, NT, preferred_element_type=F32)


def nn_dot(a, b):
    return jnp.dot(a, b, preferred_element_type=F32)


def call(body, out_shape, in_specs, scratch, flops, out_specs=None, aliases=None, limit_mb=16):
    return pl.pallas_call(
        body,
        out_shape=out_shape,
        in_specs=in_specs,
        out_specs=out_specs or jax.tree.map(lambda _: VMEM, out_shape),
        input_output_aliases=aliases or {},
        scratch_shapes=scratch,
        compiler_params=pltpu.CompilerParams(vmem_limit_bytes=limit_mb * 2**20),
        cost_estimate=pl.CostEstimate(flops=flops, bytes_accessed=2**20, transcendentals=0),
    )


def kernel_tile(scaled):
    floor = jnp.maximum(scaled, 1e-30)
    t = floor * lax.rsqrt(floor)
    return ((t + 1.0) * jnp.exp2(t * -LOG2E)).astype(BF)


def aux_rows(x):
    features, width = x.shape
    norm = jnp.sum(x * x, axis=0, keepdims=True) * (12.0 / features)
    high = norm.astype(BF).astype(F32)
    rest = norm - high
    mid = rest.astype(BF).astype(F32)
    low = rest - mid
    row = lax.broadcasted_iota(jnp.int32, (AUX, width), 0)
    norms = jnp.where(row == 0, high, jnp.where(row == 1, mid, jnp.where(row == 2, low, 0.0)))
    ones = jnp.where(row < 3, 1.0, 0.0)
    return norms, ones


def source_form(x, norms, ones):
    return jnp.concatenate([x, x, norms, ones], axis=0).astype(BF)


def target_form(x, norms, ones):
    first, second = PARTS
    return jnp.concatenate([-first * x, -second * x, ones, norms], axis=0).T.astype(BF)


def split_form(selected, features):
    return (
        selected[:features],
        selected[features : features + AUX],
        selected[features + AUX : features + 2 * AUX],
    )


def one_hot(chosen, height):
    width = chosen.shape[1]
    row = lax.broadcasted_iota(jnp.int32, (height, width), 0)
    return jnp.where(row == chosen, 1.0, 0.0).astype(BF)


def flat(table, size):
    rows, cols = table.shape
    entry = lax.broadcasted_iota(jnp.int32, (cols, size), 1)
    pick = jnp.where(entry % cols == lax.broadcasted_iota(jnp.int32, (cols, size), 0), 1.0, 0.0)
    every = nn_dot(table.astype(BF), pick.astype(BF))
    entry = lax.broadcasted_iota(jnp.int32, (rows, size), 1)
    row = lax.broadcasted_iota(jnp.int32, (rows, size), 0)
    return jnp.sum(jnp.where(entry // cols == row, every, 0.0), axis=0, keepdims=True)


def pair_list(near, far, first_leaf, rows, fixed):
    leaves, slots = near.shape
    nodes, _ = far.shape
    upper = nodes - 2
    near_size, far_size = leaves * slots, nodes * nodes
    size = -(-(near_size + far_size + upper) // 128) * 128
    rest = size - near_size - far_size
    row = lax.broadcasted_iota(jnp.int32, (nodes, nodes), 0)
    col = lax.broadcasted_iota(jnp.int32, (nodes, nodes), 1)
    seen = jnp.where(col == row + 1 - 2 * (row & 1), 1.0, 0.0)
    for s in range(far.shape[1]):
        seen = seen + jnp.where(far[:, s : s + 1] == col, 1.0, 0.0)
    here = jnp.where(near >= 0, near - (first_leaf - leaves), -1).astype(F32)
    column = lax.broadcasted_iota(jnp.int32, (1, size), 1)
    is_far = (column >= near_size) & (column < near_size + far_size)
    is_up = (column >= near_size + far_size) & (column < near_size + far_size + upper)
    near_h = jnp.concatenate([flat(here, near_size), jnp.full((1, size - near_size), -1.0, F32)], axis=1)
    times = jnp.concatenate(
        [jnp.zeros((1, near_size), F32), flat(seen, far_size + rest)], axis=1
    )
    from_far = column - near_size
    from_up = from_far - far_size
    node_first = 2 * leaves
    up_at = nodes + from_up
    sibling = up_at + 1 - 2 * (from_up & 1)
    source = jnp.where(
        is_far, node_first + from_far % nodes, jnp.where(is_up, node_first + sibling, 0)
    ).astype(F32) + jnp.where(column < near_size, near_h, 0.0)
    target = jnp.where(
        is_far, leaves + from_far // nodes, jnp.where(is_up, leaves + up_at, column // slots)
    ).astype(F32)
    times = jnp.where(is_far, times, jnp.where(is_up | (near_h >= 0), 1.0, 0.0))
    level = jnp.where(times > 0, 1.0, 0.0)
    first = jnp.where(is_far | is_up, level, 0.0)
    own = jnp.where((near_h >= leaves) & (near_h < 2 * leaves), 1.0, 0.0)
    other = level - first - own
    row = lax.broadcasted_iota(jnp.int32, (16, size), 0)
    masks = jnp.where(row == 0, first, jnp.where(row == 1, own, jnp.where(row == 2, other, 0.0)))
    before = lax.broadcasted_iota(jnp.int32, (size, size), 1) < lax.broadcasted_iota(
        jnp.int32, (size, size), 0
    )
    rank = nt_dot(masks.astype(BF), jnp.where(before, 1.0, 0.0).astype(BF))
    found = jnp.sum(masks, axis=1, keepdims=True)
    start = jnp.maximum(found[0:1] + found[1:2], float(fixed))
    place = jnp.where(other > 0, start + rank[2:3], -1.0)
    place = jnp.where(own > 0, found[0:1] + rank[1:2], place)
    place = jnp.where(first > 0, rank[0:1], place)
    slot = lax.broadcasted_iota(jnp.int32, (rows * 128, size), 0)
    slot = jnp.where(slot % 128 < ROW, slot // 128 * ROW + slot % 128, -2).astype(F32)
    hit = jnp.where(slot == place, 1.0, 0.0).astype(BF)
    parts = jnp.where(row == 0, source, jnp.where(row == 1, target, jnp.where(row == 2, times, 0.0)))
    listed = nt_dot(parts.astype(BF), hit)
    code = (listed[0:1] + 256.0 * listed[1:2] + 65536.0 * listed[2:3]).astype(jnp.int32)
    code = jnp.where(listed[2:3] > 0.5, code, leaves)
    total = jnp.broadcast_to(start + found[2:3], (1, 128)).astype(jnp.int32)
    return jnp.concatenate([code[:, 128 * r : 128 * (r + 1)] for r in range(rows)] + [total], axis=0)


def gather_kernel(
    fixed, points, charges, order, near, far, place, stacked, pairs, grid, hots, index, slots, far_slots, sems
):
    features, total = points.shape
    rows = stacked.shape[0]
    width = hots.shape[1]
    blocks = grid.shape[0]
    fetch_index = pltpu.make_async_copy(order, index, sems.at[2 * blocks])
    fetch_index.start()
    fetches = []
    for b in range(blocks):
        cols = pl.ds(b * width, width)
        into = grid.at[b, pl.ds(0, features)]
        fetches.append(pltpu.make_async_copy(points.at[:, cols], into, sems.at[2 * b]))
        into = grid.at[b, pl.ds(features, rows - features)]
        fetches.append(pltpu.make_async_copy(charges.at[:, cols], into, sems.at[2 * b + 1]))
    fetch_slots = pltpu.make_async_copy(near, slots, sems.at[2 * blocks + 1])
    fetch_slots.start()
    fetch_far = pltpu.make_async_copy(far, far_slots, sems.at[2 * blocks + 2])
    fetch_far.start()
    for fetch in fetches:
        fetch.start()
    fetch_index.wait()
    for b in range(blocks):
        hots[b] = one_hot(index[:, pl.ds(b * width, width)] & (width - 1), width)
    fetch_slots.wait()
    fetch_far.wait()
    pairs[...] = pair_list(slots[...], far_slots[...], place[0] * blocks, pairs.shape[0] - 1, fixed)
    for fetch in fetches:
        fetch.wait()

    def block(i, carry):
        for u in range(UNROLL):
            j = i * UNROLL + u
            start = pl.multiple_of(j * width, width)
            home = index[:, pl.ds(start, width)] // width
            spread = nn_dot(grid[...].reshape(blocks * rows, width), hots[j])
            found = spread[:rows]
            for b in range(1, blocks):
                found = jnp.where(home == b, spread[b * rows : (b + 1) * rows], found)
            stacked[:, pl.ds(start, width)] = found.astype(BF)
        return carry

    lax.fori_loop(0, blocks // UNROLL, block, 0)


def lift(sources, weights, target):
    kernel = kernel_tile(nn_dot(target, sources))
    sums = nt_dot(weights, kernel)
    rhs = weights.shape[0] - 16
    lifted = PAIR_GAIN * (sums[:rhs] / sums[rhs : rhs + 1])
    return kernel, lifted


def with_ones(weights):
    return jnp.concatenate([weights, jnp.ones((16, weights.shape[1]), weights.dtype)], axis=0)


def tree_kernel(
    features, stacked, skel, srcs, tgts, wtss, kernels, payload, top_tgt, joined, joined_w, hots,
):
    width = skel.shape[1]
    nodes = skel.shape[0]
    leaves = nodes + 1
    for leaf in range(leaves):
        cols = pl.ds(leaf * width, width)
        x = stacked[:features, cols].astype(F32)
        norms, ones = aux_rows(x)
        srcs[leaf] = source_form(x, norms, ones)
        tgts[leaf] = target_form(x, norms, ones)
        wtss[leaf] = stacked[features:, cols]
    live = features + 2 * AUX
    for row in range(nodes):
        slot = row % 8
        for side in range(2):
            joined[slot, :, side * width : (side + 1) * width] = srcs[2 * row + side]
            joined_w[slot, :, side * width : (side + 1) * width] = with_ones(wtss[2 * row + side])
        hots[slot] = one_hot(skel[row : row + 1, :], 2 * width)
        x, norms, ones = split_form(nn_dot(joined[slot, features:], hots[slot]), features)
        own_src = source_form(x, norms, ones)
        own_tgt = target_form(x, norms, ones)
        kernel, lifted = lift(joined[slot], joined_w[slot], own_tgt)
        kernels[row] = kernel
        own_wts = lifted.astype(BF)
        if row < nodes - 1:
            srcs[leaves + row], tgts[leaves + row], wtss[leaves + row] = own_src, own_tgt, own_wts
        else:
            payload[:live] = own_src[features:]
            payload[live:] = own_wts
            top_tgt[...] = own_tgt


def both_parts(rows):
    return jnp.concatenate([rows[: rows.shape[0] - 2 * AUX], rows], axis=0)


def chain_kernel(
    features, bit, devices, place, own, sibling, skel, _, next_own, next_tgt, half_kernel, joined, joined_w, hot
):
    live = features + 2 * AUX
    width = own.shape[1]
    joined[:, :width] = both_parts(own[:live])
    joined[:, width:] = both_parts(sibling[:live])
    joined_w[:, :width] = with_ones(own[live:])
    joined_w[:, width:] = with_ones(sibling[live:])
    chosen = skel[pl.ds(devices - (devices >> bit) + (place[0] >> (bit + 1)), 1), :]
    chosen = chosen + ((place[0] >> bit) & 1) * jnp.where(chosen < width, width, -width)
    hot[...] = one_hot(chosen, 2 * width)
    x, norms, ones = split_form(nn_dot(joined[features:], hot[...]), features)
    target = target_form(x, norms, ones)
    kernel, lifted = lift(joined[...], joined_w[...], target)
    half_kernel[...] = kernel[:, :width]
    next_tgt[...] = target
    next_own[:live] = source_form(x, norms, ones)[features:]
    next_own[live:] = lifted.astype(BF)


def pair_terms(codes, src, tgt, wts, acc, first=0):
    terms = []
    for code in codes:
        h = (code & 255) - first
        g = (code >> 8) & 255
        times = (code >> 16).astype(F32)
        kernel = kernel_tile(nn_dot(tgt[g], src[h]))
        terms.append((g, nt_dot(wts[h], kernel) * times))
    for g, term in terms:
        acc[g] = acc[g] + term


def row_pairs(pairs, row, lanes, src, tgt, wts, acc, first=0):
    codes = pairs[pl.ds(row, 1), :]
    pair_terms([codes[0, u] for u in lanes], src, tgt, wts, acc, first)


def rows_of_pairs(start, count, pairs, src, tgt, wts, acc, first=0):
    def step(i, carry):
        row_pairs(pairs, start + i, range(ROW), src, tgt, wts, acc, first)
        return carry

    lax.fori_loop(0, count, step, 0)


def own_kernel(start, count, pairs, src, tgt, wts, _, *rest):
    acc = rest[-1]
    if start == 0:
        acc[...] = jnp.zeros_like(acc)
    rows_of_pairs(start, count, pairs, src, tgt, wts, acc, (src.shape[0] + 2) // 2)


def meet_kernel(
    features, start, count, pairs, place, within, across, own_src, tgt, own_wts, _, _acc,
    acc, src, wts,
):
    leaves = src.shape[0] // 3
    width = src.shape[2]
    odd = place[0] & 1
    for halo, side in ((within, 2 - 2 * odd), (across, 2 * odd)):
        for leaf in range(leaves):
            cols = pl.ds(leaf * width, width)
            x = halo[:features, cols].astype(F32)
            at = side * leaves + leaf
            src[at] = source_form(x, *aux_rows(x))
            wts[at] = halo[features:, cols]
    src[pl.ds(leaves, leaves)] = own_src[pl.ds(0, leaves)]
    wts[pl.ds(leaves, leaves)] = own_wts[pl.ds(0, leaves)]
    rows_of_pairs(start, count, pairs, src, tgt, wts, acc)


def any_kernel(start, count, pairs, src, tgt, wts, _, _acc, acc):
    rows_of_pairs(start, count, pairs, src, tgt, wts, acc)


def finish_kernel(upper, live, taken, pairs, src, tgt, wts, order, all_acc, kernels, *rest):
    siblings = rest[:upper]
    targets = rest[upper : 2 * upper]
    half_kernels = rest[2 * upper : 3 * upper - 1]
    out, root, leaf_field, acc, spread = rest[3 * upper - 1 :]
    width = root.shape[1]
    nodes = kernels.shape[0]
    leaves = nodes + 1
    rhs = root.shape[0]

    def push(field, kernel):
        sums = nn_dot(with_ones(field.astype(BF)), kernel)
        return sums[:rhs] / sums[rhs : rhs + 1]

    acc[...] = all_acc[pl.ds(0, leaves)]
    coupled = []
    for bit in range(upper):
        kernel = kernel_tile(nn_dot(targets[bit][...], both_parts(siblings[bit][:live])))
        coupled.append(nt_dot(siblings[bit][live:], kernel))
    field = coupled[upper - 1]
    for bit in range(upper - 2, -1, -1):
        field = coupled[bit] + push(field, half_kernels[bit][...])
    root[...] = field
    fields = {nodes - 1: field}
    for row in range(nodes - 1, -1, -1):
        pushed = push(fields[row], kernels[row])
        for side in range(2):
            below = 2 * row + side
            passed = pushed[:, side * width : (side + 1) * width]
            if below < leaves:
                leaf_field[below] = passed
            else:
                fields[below - leaves] = all_acc[below] + passed
    row_pairs(pairs, taken, range(2 * BLOCK), src, tgt, wts, acc)
    last = pairs.shape[0] - 1
    total = pairs[last : last + 1, :][0, 0]

    def more(row, carry):
        for first in range(0, ROW, BLOCK):
            fresh = total > row * ROW + first
            if first < 2 * BLOCK:
                fresh = fresh & (row > taken)

            @pl.when(fresh)
            def _():
                row_pairs(pairs, row, range(first, first + BLOCK), src, tgt, wts, acc)

        return carry

    lax.fori_loop(taken, (total + (ROW - 1)) // ROW, more, 0)
    spread[...] = jnp.zeros_like(spread)
    span = UNROLL * width

    def scatter(i, carry):
        index = order[:, pl.ds(pl.multiple_of(i * span, span), span)]
        home = index // width
        hot_t = one_hot(index & (width - 1), width)
        at = [i * UNROLL + u for u in range(UNROLL)]
        rows = jnp.concatenate([acc[leaf] + leaf_field[leaf] for leaf in at], axis=1)
        high = rows.astype(BF)
        low = (rows - high.astype(F32)).astype(BF)
        both = jnp.concatenate([high, low], axis=0)
        stack = []
        for b in range(leaves):
            mask = jnp.where(home == b, 1.0, 0.0).astype(BF)
            stack.append(both * mask)
        spread[...] += nt_dot(jnp.concatenate(stack, axis=0), hot_t)
        return carry

    lax.fori_loop(0, leaves // UNROLL, scatter, 0)
    for b in range(leaves):
        at = b * 2 * rhs
        out[:, pl.ds(b * width, width)] = spread[pl.ds(at, rhs)] + spread[pl.ds(at + rhs, rhs)]


def local(points, charges, leaf_order, near_list, far_list, local_skel, upper_skel):
    features, total = points.shape
    rhs = charges.shape[0]
    leaves, _ = near_list.shape
    width = local_skel.shape[1]
    nodes = local_skel.shape[0]
    devices = lax.axis_size("leaf")
    upper = devices.bit_length() - 1
    position = lax.axis_index("leaf")
    live = features + 2 * AUX
    depth = features + live
    rows = features + rhs
    assert 24 / features == sum(PARTS)
    shape = jax.ShapeDtypeStruct
    place = jnp.reshape(position, (1,)).astype(jnp.int32)

    half = leaves // 2
    fixed = sum(OWN_ROWS) * ROW
    most = near_list.size + max(half * half + half - 2, fixed)
    list_rows = max(-(-most // ROW), sum(OWN_ROWS + ANY_ROWS) + 1)
    stacked, pairs = call(
        functools.partial(gather_kernel, fixed),
        (shape((rows, total), BF), shape((list_rows + 1, 128), jnp.int32)),
        [HBM] * 5 + [SMEM],
        [
            pltpu.VMEM((leaves, rows, width), BF),
            pltpu.VMEM((leaves, width, width), BF),
            pltpu.VMEM((1, total), jnp.int32),
            pltpu.VMEM(near_list.shape, jnp.int32),
            pltpu.VMEM(far_list.shape, jnp.int32),
            pltpu.SemaphoreType.DMA((2 * leaves + 3,)),
        ],
        10**10,
        limit_mb=63,
    )(points, charges, leaf_order, near_list, far_list, place)
    within = lax.ppermute(stacked, "leaf", [(i, i ^ 1) for i in range(devices)])
    across = lax.ppermute(
        stacked, "leaf", [(i, i + 1 if i % 2 else i - 1) for i in range(1, devices - 1)]
    )
    known = leaves + nodes - 1
    srcs, tgts, wtss, kernels, own, own_tgt = call(
        functools.partial(tree_kernel, features),
        (
            shape((known, depth, width), BF),
            shape((known, width, depth), BF),
            shape((known, rhs, width), BF),
            shape((nodes, width, 2 * width), BF),
            shape((live + rhs, width), BF),
            shape((width, depth), BF),
        ),
        [VMEM] * 2,
        [
            pltpu.VMEM((8, depth, 2 * width), BF),
            pltpu.VMEM((8, rhs + 16, 2 * width), BF),
            pltpu.VMEM((8, 2 * width, width), BF),
        ],
        10**10,
    )(stacked, local_skel)

    def own_part(start, count, after, acc):
        return call(
            functools.partial(own_kernel, start, count),
            shape((known, rhs, width), F32),
            [VMEM] * 4 + [ANY] + [VMEM] * (start > 0),
            [],
            10**10,
            aliases={5: 0} if start else None,
        )(pairs, srcs, tgts, wtss, after, *([acc] if start else []))

    def meet_part(start, count, after, acc):
        return call(
            functools.partial(meet_kernel, features, start, count),
            (
                shape((known, rhs, width), F32),
                shape((3 * leaves, depth, width), BF),
                shape((3 * leaves, rhs, width), BF),
            ),
            [VMEM, SMEM] + [VMEM] * 5 + [ANY, VMEM],
            [],
            10**10,
            aliases={8: 0},
        )(pairs, place, within, across, srcs, tgts, wtss, after, acc)

    def any_part(start, count, after, acc):
        return call(
            functools.partial(any_kernel, start, count),
            shape((known, rhs, width), F32),
            [VMEM] * 4 + [ANY, VMEM],
            [],
            10**10,
            aliases={5: 0},
        )(pairs, all_src, tgts, all_wts, after, acc)

    siblings, targets, half_kernels = [], [], []
    acc = all_src = all_wts = None
    taken = 0
    for bit in range(upper):
        sibling = lax.ppermute(own, "leaf", [(i, i ^ (1 << bit)) for i in range(devices)])
        part = bit - len(OWN_ROWS)
        if part < 0:
            count = OWN_ROWS[bit]
            acc = own_part(taken, count, own, acc)
        elif part < len(ANY_ROWS):
            count = ANY_ROWS[part]
            if part == 0:
                acc, all_src, all_wts = meet_part(taken, count, own, acc)
            else:
                acc = any_part(taken, count, own, acc)
        else:
            count = 0
        taken += count
        siblings.append(sibling)
        targets.append(own_tgt)
        if bit == upper - 1:
            break
        own, own_tgt, half_kernel = call(
            functools.partial(chain_kernel, features, bit, devices),
            (
                shape((live + rhs, width), BF),
                shape((width, depth), BF),
                shape((width, width), BF),
            ),
            [SMEM] + [VMEM] * 3 + [ANY],
            [
                pltpu.VMEM((depth, 2 * width), BF),
                pltpu.VMEM((rhs + 16, 2 * width), BF),
                pltpu.VMEM((2 * width, width), BF),
            ],
            10**8,
        )(place, own, sibling, upper_skel, acc)
        half_kernels.append(half_kernel)

    potentials, root = call(
        functools.partial(finish_kernel, upper, live, taken),
        (shape((rhs, total), F32), shape((rhs, width), F32)),
        [VMEM] * (7 + 3 * upper - 1),
        [
            pltpu.VMEM((leaves, rhs, width), F32),
            pltpu.VMEM((leaves, rhs, width), F32),
            pltpu.VMEM((leaves * 2 * rhs, width), F32),
        ],
        10**10,
    )(pairs, all_src, tgts, all_wts, leaf_order, acc, kernels, *siblings, *targets, *half_kernels)
    return (potentials, root[None])


def solution(mesh):
    placed = (
        P(None, "leaf"),
        P(None, "leaf"),
        P("leaf", None),
        P("leaf", None),
        P("leaf", None),
        P("leaf", None),
        P(),
    )
    return jax.shard_map(
        local,
        mesh=mesh,
        in_specs=placed,
        out_specs=(P(None, "leaf"), P("leaf", None, None)),
        check_vma=False,
    )
```

profile of v0, /device:TPU:0, one launch (start us, length us, event | category | flops | bytes accessed | tf_op | source)
XLA Modules:
  0.0 62.2 jit_solution(15478889435284942214)
XLA Ops:
  0.6 0.0 copy-start.2
  0.6 7.1 %shard_map.86 = (bf16[96,4096]{1,0:T(8,128)(2,1)}, s32[13,128]{1,0:T(8,128)}) custom-call(bf16[64,4096]{1,0:T(8,128)(2,1)} %points.1, bf16[32,4096]{1,0:T(8,128)(2,1)} %charges.1, s32[1,4096]{1,0:T(1,128)} %order.3, s32[16,16]{1,0:T(8,128)} %near.1, s32[8,8]{1,0:T(8,128)} %far.1, s32[1]{0:T(128)} %bitcast.place), custom_call_target="tpu_custom_call" | custom-call | flops 10000000000 | bytes 1048576 | tf_op jit(solution)/shard_map/pallas_call | solution.py:426
  7.7 0.7 %collective-permute-start.1 = (bf16[96,4096]{1,0:T(8,128)(2,1)}, bf16[96,4096]{1,0:T(8,128)(2,1)S(1)}, u32[]{:S(2)}, u32[]{:S(2)}) collective-permute-start(bf16[96,4096]{1,0:T(8,128)(2,1)} %get-tuple-element.28.stacked), channel_id=1, source_target_pairs={{1,2},{2,1},{3,4},{4,3},{5,6},{6,5},{7,8},{8,7},{9,10},{10,9},{11,... | collective-permute-start | bytes 2359304 | tf_op jit(solution)/shard_map/ppermute | solution.py:442
  8.5 4.3 %collective-permute-start = (bf16[96,4096]{1,0:T(8,128)(2,1)}, bf16[96,4096]{1,0:T(8,128)(2,1)S(1)}, u32[]{:S(2)}, u32[]{:S(2)}) collective-permute-start(bf16[96,4096]{1,0:T(8,128)(2,1)} %get-tuple-element.28.stacked), channel_id=1, source_target_pairs={{0,1},{1,0},{2,3},{3,2},{4,5},{5,4},{6,7},{7,6},{8,9},{9,8},{10,11... | collective-permute-start | bytes 2359304 | tf_op jit(solution)/shard_map/ppermute | solution.py:441
  12.8 1.1 %copy-done.1 = bf16[96,4096]{1,0:T(8,128)(2,1)S(1)} copy-done((bf16[96,4096]{1,0:T(8,128)(2,1)S(1)}, bf16[96,4096]{1,0:T(8,128)(2,1)}, u32[]{:S(2)}) %copy-start.1) | copy-done | bytes 786456
  13.9 6.4 %shard_map.87 = (bf16[30,144,256]{2,1,0:T(8,128)(2,1)S(1)}, bf16[30,256,144]{2,1,0:T(8,128)(2,1)S(1)}, bf16[30,32,256]{2,1,0:T(8,128)(2,1)S(1)}, bf16[15,256,512...) custom-call(bf16[96,4096]{1,0:T(8,128)(2,1)S(1)} %copy-done.1, s32[15,256]{1,0:T(8,128)S(1)} %copy-done.2), custom_call_target="tpu_custom_call" | custom-call | flops 10000000000 | bytes 1048576 | tf_op jit(solution)/shard_map/pallas_call | solution.py:446
  20.3 0.1 collective-permute-start.2
  20.4 0.0 copy-done.4
  20.4 0.0 copy-start
  20.4 6.6 %shard_map.88._.rest_0_ = f32[30,32,256]{2,1,0:T(8,128)S(1)} custom-call(s32[13,128]{1,0:T(8,128)S(1)} %copy-done.4, bf16[30,144,256]{2,1,0:T(8,128)(2,1)S(1)} %get-tuple-element.29.src.own_src, bf16[30,256,144]{2,1,0:T(8,128)(2,1)S(1)} %get-tuple-element.30.tgt, bf16[30,32,256]{2,1,0:T(8,128)(2,1)S(1)} %get-tuple-element.31.wts.own_wts, ...), custom_call_target="tpu_custom_call" | custom-call | flops 10000000000 | bytes 1048576 | tf_op jit(solution)/shard_map/pallas_call | solution.py:466
  27.0 0.0 collective-permute-done.2.sibling.rest_0_
  27.1 0.7 %shard_map.89 = (bf16[112,256]{1,0:T(8,128)(2,1)S(1)}, bf16[256,144]{1,0:T(8,128)(2,1)S(1)}, bf16[256,256]{1,0:T(8,128)(2,1)S(1)}) custom-call(s32[1]{0:T(128)} %bitcast.place, bf16[112,256]{1,0:T(8,128)(2,1)S(1)} %get-tuple-element.32._.own, bf16[112,256]{1,0:T(8,128)(2,1)S(1)} %collective-permute-done.2.sibling.rest_0_, s32[30,256]{1,0:T(8,128)S(1)} %copy-done, ...), custom_call_target="tpu_custom_call" | custom-call | flops 100000000 | bytes 1048576 | tf_op jit(solution)/shard_map/pallas_call | solution.py:521
  27.8 1.6 %collective-permute-start.3 = (bf16[112,256]{1,0:T(8,128)(2,1)S(1)}, bf16[112,256]{1,0:T(8,128)(2,1)S(1)}, u32[]{:S(2)}, u32[]{:S(2)}) collective-permute-start(bf16[112,256]{1,0:T(8,128)(2,1)S(1)} %get-tuple-element.33._.own), channel_id=1, source_target_pairs={{0,2},{1,3},{2,0},{3,1},{4,6},{5,7},{6,4},{7,5},{8,10},{9,11},{10,... | collective-permute-start | bytes 172040 | tf_op jit(solution)/shard_map/ppermute | solution.py:503
  29.3 6.5 %shard_map.90._._acc = f32[30,32,256]{2,1,0:T(8,128)S(1)} custom-call(s32[13,128]{1,0:T(8,128)S(1)} %copy-done.4, bf16[30,144,256]{2,1,0:T(8,128)(2,1)S(1)} %get-tuple-element.29.src.own_src, bf16[30,256,144]{2,1,0:T(8,128)(2,1)S(1)} %get-tuple-element.30.tgt, ...), custom_call_target="tpu_custom_call", output_to_operand_aliasing={{}: (5, {})} | custom-call | flops 10000000000 | bytes 1048576 | tf_op jit(solution)/shard_map/pallas_call | solution.py:466
  35.9 0.0 collective-permute-done.3.sibling.rest_1_
  35.9 0.7 %shard_map.91 = (bf16[112,256]{1,0:T(8,128)(2,1)S(1)}, bf16[256,144]{1,0:T(8,128)(2,1)S(1)}, bf16[256,256]{1,0:T(8,128)(2,1)S(1)}) custom-call(s32[1]{0:T(128)} %bitcast.place, bf16[112,256]{1,0:T(8,128)(2,1)S(1)} %get-tuple-element.33._.own, bf16[112,256]{1,0:T(8,128)(2,1)S(1)} %collective-permute-done.3.sibling.rest_1_, s32[30,256]{1,0:T(8,128)S(1)} %copy-done, ...), custom_call_target="tpu_custom_call" | custom-call | flops 100000000 | bytes 1048576 | tf_op jit(solution)/shard_map/pallas_call | solution.py:521
  36.6 1.6 %collective-permute-start.4 = (bf16[112,256]{1,0:T(8,128)(2,1)S(1)}, bf16[112,256]{1,0:T(8,128)(2,1)S(1)}, u32[]{:S(2)}, u32[]{:S(2)}) collective-permute-start(bf16[112,256]{1,0:T(8,128)(2,1)S(1)} %get-tuple-element.34._.own), channel_id=1, source_target_pairs={{0,4},{1,5},{2,6},{3,7},{4,0},{5,1},{6,2},{7,3},{8,12},{9,13},{10,... | collective-permute-start | bytes 172040 | tf_op jit(solution)/shard_map/ppermute | solution.py:503
  38.2 0.0 collective-permute-done.1.across
  38.2 0.0 collective-permute-done.within
  38.2 3.5 %shard_map.92 = (f32[30,32,256]{2,1,0:T(8,128)S(1)}, bf16[48,144,256]{2,1,0:T(8,128)(2,1)S(1)}, bf16[48,32,256]{2,1,0:T(8,128)(2,1)S(1)}) custom-call(s32[13,128]{1,0:T(8,128)S(1)} %copy-done.4, s32[1]{0:T(128)} %bitcast.place, bf16[96,4096]{1,0:T(8,128)(2,1)S(1)} %collective-permute-done.within, ...), custom_call_target="tpu_custom_call", output_to_operand_aliasing={{0}: (8, {})} | custom-call | flops 10000000000 | bytes 1048576 | tf_op jit(solution)/shard_map/pallas_call | solution.py:476
  41.7 0.0 collective-permute-done.4.sibling.rest_2_
  41.7 0.7 %shard_map.93 = (bf16[112,256]{1,0:T(8,128)(2,1)S(1)}, bf16[256,144]{1,0:T(8,128)(2,1)S(1)}, bf16[256,256]{1,0:T(8,128)(2,1)S(1)}) custom-call(s32[1]{0:T(128)} %bitcast.place, bf16[112,256]{1,0:T(8,128)(2,1)S(1)} %get-tuple-element.34._.own, bf16[112,256]{1,0:T(8,128)(2,1)S(1)} %collective-permute-done.4.sibling.rest_2_, s32[30,256]{1,0:T(8,128)S(1)} %copy-done, ...), custom_call_target="tpu_custom_call" | custom-call | flops 100000000 | bytes 1048576 | tf_op jit(solution)/shard_map/pallas_call | solution.py:521
  42.4 1.6 %collective-permute-start.5 = (bf16[112,256]{1,0:T(8,128)(2,1)S(1)}, bf16[112,256]{1,0:T(8,128)(2,1)S(1)}, u32[]{:S(2)}, u32[]{:S(2)}) collective-permute-start(bf16[112,256]{1,0:T(8,128)(2,1)S(1)} %get-tuple-element.38._.own), channel_id=1, source_target_pairs={{0,8},{1,9},{2,10},{3,11},{4,12},{5,13},{6,14},{7,15},{8,0},{9,1},... | collective-permute-start | bytes 172040 | tf_op jit(solution)/shard_map/ppermute | solution.py:503
  44.1 3.2 %shard_map.94._._acc = f32[30,32,256]{2,1,0:T(8,128)S(1)} custom-call(s32[13,128]{1,0:T(8,128)S(1)} %copy-done.4, bf16[48,144,256]{2,1,0:T(8,128)(2,1)S(1)} %get-tuple-element.35.src, bf16[30,256,144]{2,1,0:T(8,128)(2,1)S(1)} %get-tuple-element.30.tgt, bf16[48,32,256]{2,1,0:T(8,128)(2,1)S(1)} %get-tuple-element.36.wts, ...), custom_call_target="tpu_custom_call", output_to_operand_aliasing={{}: (5, {})} | custom-call | flops 10000000000 | bytes 1048576 | tf_op jit(solution)/shard_map/pallas_call | solution.py:490
  47.2 0.0 collective-permute-done.5.sibling.rest_3_
  47.2 0.7 %shard_map.95 = (bf16[112,256]{1,0:T(8,128)(2,1)S(1)}, bf16[256,144]{1,0:T(8,128)(2,1)S(1)}, bf16[256,256]{1,0:T(8,128)(2,1)S(1)}) custom-call(s32[1]{0:T(128)} %bitcast.place, bf16[112,256]{1,0:T(8,128)(2,1)S(1)} %get-tuple-element.38._.own, bf16[112,256]{1,0:T(8,128)(2,1)S(1)} %collective-permute-done.5.sibling.rest_3_, s32[30,256]{1,0:T(8,128)S(1)} %copy-done, ...), custom_call_target="tpu_custom_call" | custom-call | flops 100000000 | bytes 1048576 | tf_op jit(solution)/shard_map/pallas_call | solution.py:521
  48.0 0.0 copy-start.3
  48.0 2.1 %collective-permute-start.6 = (bf16[112,256]{1,0:T(8,128)(2,1)S(1)}, bf16[112,256]{1,0:T(8,128)(2,1)S(1)}, u32[]{:S(2)}, u32[]{:S(2)}) collective-permute-start(bf16[112,256]{1,0:T(8,128)(2,1)S(1)} %get-tuple-element.39._), channel_id=1, source_target_pairs={{0,16},{1,17},{2,18},{3,19},{4,20},{5,21},{6,22},{7,23},{8,24},{9,... | collective-permute-start | bytes 172040 | tf_op jit(solution)/shard_map/ppermute | solution.py:503
  50.0 3.2 %shard_map.96.all_acc = f32[30,32,256]{2,1,0:T(8,128)S(1)} custom-call(s32[13,128]{1,0:T(8,128)S(1)} %copy-done.4, bf16[48,144,256]{2,1,0:T(8,128)(2,1)S(1)} %get-tuple-element.35.src, bf16[30,256,144]{2,1,0:T(8,128)(2,1)S(1)} %get-tuple-element.30.tgt, bf16[48,32,256]{2,1,0:T(8,128)(2,1)S(1)} %get-tuple-element.36.wts, ...), custom_call_target="tpu_custom_call", output_to_operand_aliasing={{}: (5, {})} | custom-call | flops 10000000000 | bytes 1048576 | tf_op jit(solution)/shard_map/pallas_call | solution.py:490
  53.2 0.5 collective-permute-done.6.rest_4_
  53.7 0.0 copy-done.3
  53.7 8.4 %shard_map.97 = (f32[32,4096]{1,0:T(8,128)}, f32[32,256]{1,0:T(8,128)}) custom-call(s32[13,128]{1,0:T(8,128)S(1)} %copy-done.4, bf16[48,144,256]{2,1,0:T(8,128)(2,1)S(1)} %get-tuple-element.35.src, bf16[30,256,144]{2,1,0:T(8,128)(2,1)S(1)} %get-tuple-element.30.tgt, bf16[48,32,256]{2,1,0:T(8,128)(2,1)S(1)} %get-tuple-element.36.wts, ...), custom_call_target="tpu_custom_call" | custom-call | flops 10000000000 | bytes 1048576 | tf_op jit(solution)/shard_map/pallas_call | solution.py:538
  (4 shorter events, 0.0 us)
Async XLA Ops:
  0.6 12.2 %copy-start.2 = (s32[15,256]{1,0:T(8,128)S(1)}, s32[15,256]{1,0:T(8,128)}, u32[]{:S(2)}) copy-start(s32[15,256]{1,0:T(8,128)} %skel.5) | copy-start | bytes 46084
  7.7 30.5 %collective-permute-start.1 = (bf16[96,4096]{1,0:T(8,128)(2,1)}, bf16[96,4096]{1,0:T(8,128)(2,1)S(1)}, u32[]{:S(2)}, u32[]{:S(2)}) collective-permute-start(bf16[96,4096]{1,0:T(8,128)(2,1)} %get-tuple-element.28.stacked), channel_id=1, source_target_pairs={{1,2},{2,1},{3,4},{4,3},{5,6},{6,5},{7,8},{8,7},{9,10},{10,9},{11,... | collective-permute-start | bytes 2359304 | tf_op jit(solution)/shard_map/ppermute | solution.py:442
  8.5 29.7 %collective-permute-start = (bf16[96,4096]{1,0:T(8,128)(2,1)}, bf16[96,4096]{1,0:T(8,128)(2,1)S(1)}, u32[]{:S(2)}, u32[]{:S(2)}) collective-permute-start(bf16[96,4096]{1,0:T(8,128)(2,1)} %get-tuple-element.28.stacked), channel_id=1, source_target_pairs={{0,1},{1,0},{2,3},{3,2},{4,5},{5,4},{6,7},{7,6},{8,9},{9,8},{10,11... | collective-permute-start | bytes 2359304 | tf_op jit(solution)/shard_map/ppermute | solution.py:441
  12.8 1.1 %copy-start.1 = (bf16[96,4096]{1,0:T(8,128)(2,1)S(1)}, bf16[96,4096]{1,0:T(8,128)(2,1)}, u32[]{:S(2)}) copy-start(bf16[96,4096]{1,0:T(8,128)(2,1)} %get-tuple-element.28.stacked) | copy-start | bytes 2359300
  13.9 6.5 %copy-start.4 = (s32[13,128]{1,0:T(8,128)S(1)}, s32[13,128]{1,0:T(8,128)}, u32[]{:S(2)}) copy-start(s32[13,128]{1,0:T(8,128)} %get-tuple-element.27.pairs) | copy-start | bytes 19972
  20.3 6.7 %collective-permute-start.2 = (bf16[112,256]{1,0:T(8,128)(2,1)S(1)}, bf16[112,256]{1,0:T(8,128)(2,1)S(1)}, u32[]{:S(2)}, u32[]{:S(2)}) collective-permute-start(bf16[112,256]{1,0:T(8,128)(2,1)S(1)} %get-tuple-element.32._.own), channel_id=1, source_target_pairs={{0,1},{1,0},{2,3},{3,2},{4,5},{5,4},{6,7},{7,6},{8,9},{9,8},{10,11... | collective-permute-start | bytes 172040 | tf_op jit(solution)/shard_map/ppermute | solution.py:503
  20.4 6.6 %copy-start = (s32[30,256]{1,0:T(8,128)S(1)}, s32[30,256]{1,0:T(8,128)}, u32[]{:S(2)}) copy-start(s32[30,256]{1,0:T(8,128)} %skel.9) | copy-start | bytes 92164
  27.8 8.1 %collective-permute-start.3 = (bf16[112,256]{1,0:T(8,128)(2,1)S(1)}, bf16[112,256]{1,0:T(8,128)(2,1)S(1)}, u32[]{:S(2)}, u32[]{:S(2)}) collective-permute-start(bf16[112,256]{1,0:T(8,128)(2,1)S(1)} %get-tuple-element.33._.own), channel_id=1, source_target_pairs={{0,2},{1,3},{2,0},{3,1},{4,6},{5,7},{6,4},{7,5},{8,10},{9,11},{10,... | collective-permute-start | bytes 172040 | tf_op jit(solution)/shard_map/ppermute | solution.py:503
  36.6 5.1 %collective-permute-start.4 = (bf16[112,256]{1,0:T(8,128)(2,1)S(1)}, bf16[112,256]{1,0:T(8,128)(2,1)S(1)}, u32[]{:S(2)}, u32[]{:S(2)}) collective-permute-start(bf16[112,256]{1,0:T(8,128)(2,1)S(1)} %get-tuple-element.34._.own), channel_id=1, source_target_pairs={{0,4},{1,5},{2,6},{3,7},{4,0},{5,1},{6,2},{7,3},{8,12},{9,13},{10,... | collective-permute-start | bytes 172040 | tf_op jit(solution)/shard_map/ppermute | solution.py:503
  42.4 4.8 %collective-permute-start.5 = (bf16[112,256]{1,0:T(8,128)(2,1)S(1)}, bf16[112,256]{1,0:T(8,128)(2,1)S(1)}, u32[]{:S(2)}, u32[]{:S(2)}) collective-permute-start(bf16[112,256]{1,0:T(8,128)(2,1)S(1)} %get-tuple-element.38._.own), channel_id=1, source_target_pairs={{0,8},{1,9},{2,10},{3,11},{4,12},{5,13},{6,14},{7,15},{8,0},{9,1},... | collective-permute-start | bytes 172040 | tf_op jit(solution)/shard_map/ppermute | solution.py:503
  48.0 5.8 %copy-start.3 = (s32[1,4096]{1,0:T(1,128)S(1)}, s32[1,4096]{1,0:T(1,128)}, u32[]{:S(2)}) copy-start(s32[1,4096]{1,0:T(1,128)} %order.3) | copy-start | bytes 49156
  48.0 5.8 %collective-permute-start.6 = (bf16[112,256]{1,0:T(8,128)(2,1)S(1)}, bf16[112,256]{1,0:T(8,128)(2,1)S(1)}, u32[]{:S(2)}, u32[]{:S(2)}) collective-permute-start(bf16[112,256]{1,0:T(8,128)(2,1)S(1)} %get-tuple-element.39._), channel_id=1, source_target_pairs={{0,16},{1,17},{2,18},{3,19},{4,20},{5,21},{6,22},{7,23},{8,24},{9,... | collective-permute-start | bytes 172040 | tf_op jit(solution)/shard_map/ppermute | solution.py:503
where the time goes:
time: 62.4 us; the launch traced here: 62.2 us
  Pallas kernels  47.7 us (76%)
  starting transfers between devices  12 us (19%)
  local copies, waits for them, and re-layouts  1.15 us (2%)
  between operations  0.77 us (1%)
    pallas_call x2, Pallas kernels, own_part(): call(functools.partial(own_kernel, start, count), shape((known, rhs, widt...  13.2 us
    pallas_call x1, Pallas kernels, local(): call(functools.partial(finish_kernel, upper, live, taken), (shape((rhs, t...  8.43 us
    pallas_call x1, Pallas kernels, local(): call(functools.partial(gather_kernel, fixed), (shape((rows, total), BF),...  7.1 us
    ppermute x5, starting transfers between devices, local(): lax.ppermute(own, 'leaf', [(i, i ^ 1 << bit) for i in range(devices)])  6.93 us
    pallas_call x1, Pallas kernels, local(): call(functools.partial(tree_kernel, features), (shape((known, depth, widt...  6.41 us
    pallas_call x2, Pallas kernels, any_part(): call(functools.partial(any_kernel, start, count), shape((known, rhs, widt...  6.34 us
    ppermute x1, starting transfers between devices, local(): within = lax.ppermute(stacked, 'leaf', [(i, i ^ 1) for i in range(devices)])  4.32 us
    pallas_call x1, Pallas kernels, meet_part(): call(functools.partial(meet_kernel, features, start, count), (shape((know...  3.46 us
  transfers between devices with their start and end apart: 7, of which 1 were waited for; matrix products, arithmetic and copies ran while one was open for 0% of the time, Pallas kernels for 49%

commit v1 on v0

--- a/solution.py
+++ b/solution.py
@@ -18,7 +18,7 @@
 ROW, BLOCK = 36, 12
 OWN_ROWS = (2, 2)
 ANY_ROWS = (1, 1, 1)
-UNROLL = 4
+UNROLL = 8
 VMEM = pl.BlockSpec(memory_space=pltpu.VMEM)
 SMEM = pl.BlockSpec(memory_space=pltpu.SMEM)
 HBM = pl.BlockSpec(memory_space=pltpu.HBM)
@@ -202,12 +202,10 @@
     lax.fori_loop(0, blocks // UNROLL, block, 0)
 
 
-def lift(sources, weights, target):
-    kernel = kernel_tile(nn_dot(target, sources))
+def lift(weights, kernel):
     sums = nt_dot(weights, kernel)
     rhs = weights.shape[0] - 16
-    lifted = PAIR_GAIN * (sums[:rhs] / sums[rhs : rhs + 1])
-    return kernel, lifted
+    return PAIR_GAIN * (sums[:rhs] / sums[rhs : rhs + 1])
 
 
 def with_ones(weights):
@@ -229,23 +227,28 @@
         wtss[leaf] = stacked[features:, cols]
     live = features + 2 * AUX
     for row in range(nodes):
-        slot = row % 8
         for side in range(2):
-            joined[slot, :, side * width : (side + 1) * width] = srcs[2 * row + side]
-            joined_w[slot, :, side * width : (side + 1) * width] = with_ones(wtss[2 * row + side])
-        hots[slot] = one_hot(skel[row : row + 1, :], 2 * width)
-        x, norms, ones = split_form(nn_dot(joined[slot, features:], hots[slot]), features)
+            joined[row, :, side * width : (side + 1) * width] = srcs[2 * row + side]
+        hots[row] = one_hot(skel[row : row + 1, :], 2 * width)
+        x, norms, ones = split_form(nn_dot(joined[row, features:], hots[row]), features)
         own_src = source_form(x, norms, ones)
         own_tgt = target_form(x, norms, ones)
-        kernel, lifted = lift(joined[slot], joined_w[slot], own_tgt)
-        kernels[row] = kernel
-        own_wts = lifted.astype(BF)
         if row < nodes - 1:
-            srcs[leaves + row], tgts[leaves + row], wtss[leaves + row] = own_src, own_tgt, own_wts
+            srcs[leaves + row], tgts[leaves + row] = own_src, own_tgt
         else:
             payload[:live] = own_src[features:]
+            top_tgt[...] = own_tgt
+    for row in range(nodes):
+        target = tgts[leaves + row] if row < nodes - 1 else top_tgt[...]
+        kernels[row] = kernel_tile(nn_dot(target, joined[row]))
+    for row in range(nodes):
+        for side in range(2):
+            joined_w[row, :, side * width : (side + 1) * width] = with_ones(wtss[2 * row + side])
+        own_wts = lift(joined_w[row], kernels[row]).astype(BF)
+        if row < nodes - 1:
+            wtss[leaves + row] = own_wts
+        else:
             payload[live:] = own_wts
-            top_tgt[...] = own_tgt
 
 
 def both_parts(rows):
@@ -266,7 +269,8 @@
     hot[...] = one_hot(chosen, 2 * width)
     x, norms, ones = split_form(nn_dot(joined[features:], hot[...]), features)
     target = target_form(x, norms, ones)
-    kernel, lifted = lift(joined[...], joined_w[...], target)
+    kernel = kernel_tile(nn_dot(target, joined[...]))
+    lifted = lift(joined_w[...], kernel)
     half_kernel[...] = kernel[:, :width]
     next_tgt[...] = target
     next_own[:live] = source_form(x, norms, ones)[features:]
@@ -455,9 +459,9 @@
         ),
         [VMEM] * 2,
         [
-            pltpu.VMEM((8, depth, 2 * width), BF),
-            pltpu.VMEM((8, rhs + 16, 2 * width), BF),
-            pltpu.VMEM((8, 2 * width, width), BF),
+            pltpu.VMEM((nodes, depth, 2 * width), BF),
+            pltpu.VMEM((nodes, rhs + 16, 2 * width), BF),
+            pltpu.VMEM((nodes, 2 * width, width), BF),
         ],
         10**10,
     )(stacked, local_skel)

time: 62.4 us -> 59.6 us (0.955)
  Pallas kernels: 47.7 us -> 44.8 us
    pallas_call x1, Pallas kernels: 6.41 us -> 4.43 us  [local(): call(functools.partial(tree_kernel, features), (shape((known, depth, widt...]
  transfers between devices with their start and end apart: 7 -> 7, of which waited for: 1 -> 1; matrix products, arithmetic and copies ran while one was open for 0% -> 0% of each run, Pallas kernels for 49% -> 48%
where the time goes in v1:
time: 59.6 us; the launch traced here: 59.4 us
  Pallas kernels  44.8 us (75%)
  starting transfers between devices  12.1 us (20%)
  local copies, waits for them, and re-layouts  1.15 us (2%)
  between operations  0.77 us (1%)
    pallas_call x2, Pallas kernels, own_part(): call(functools.partial(own_kernel, start, count), shape((known, rhs, widt...  13 us
    pallas_call x1, Pallas kernels, local(): call(functools.partial(finish_kernel, upper, live, taken), (shape((rhs, t...  8.01 us
    ppermute x5, starting transfers between devices, local(): lax.ppermute(own, 'leaf', [(i, i ^ 1 << bit) for i in range(devices)])  6.93 us
    pallas_call x1, Pallas kernels, local(): call(functools.partial(gather_kernel, fixed), (shape((rows, total), BF),...  6.76 us
    pallas_call x2, Pallas kernels, any_part(): call(functools.partial(any_kernel, start, count), shape((known, rhs, widt...  6.34 us
    pallas_call x1, Pallas kernels, local(): call(functools.partial(tree_kernel, features), (shape((known, depth, widt...  4.43 us
    ppermute x1, starting transfers between devices, local(): within = lax.ppermute(stacked, 'leaf', [(i, i ^ 1) for i in range(devices)])  4.31 us
    pallas_call x1, Pallas kernels, meet_part(): call(functools.partial(meet_kernel, features, start, count), (shape((know...  3.46 us
  transfers between devices with their start and end apart: 7, of which 1 were waited for; matrix products, arithmetic and copies ran while one was open for 0% of the time, Pallas kernels for 48%

profile of v1, /device:TPU:0, one launch (start us, length us, event | category | flops | bytes accessed | tf_op | source)
XLA Modules:
  0.0 59.4 jit_solution(10646828437621613006)
XLA Ops:
  0.6 0.0 copy-start.2
  0.6 6.8 %shard_map.86 = (bf16[96,4096]{1,0:T(8,128)(2,1)}, s32[13,128]{1,0:T(8,128)}) custom-call(bf16[64,4096]{1,0:T(8,128)(2,1)} %points.1, bf16[32,4096]{1,0:T(8,128)(2,1)} %charges.1, s32[1,4096]{1,0:T(1,128)} %order.3, s32[16,16]{1,0:T(8,128)} %near.1, s32[8,8]{1,0:T(8,128)} %far.1, s32[1]{0:T(128)} %bitcast.place), custom_call_target="tpu_custom_call" | custom-call | flops 10000000000 | bytes 1048576 | tf_op jit(solution)/shard_map/pallas_call | solution.py:430
  7.4 0.9 %collective-permute-start.1 = (bf16[96,4096]{1,0:T(8,128)(2,1)}, bf16[96,4096]{1,0:T(8,128)(2,1)S(1)}, u32[]{:S(2)}, u32[]{:S(2)}) collective-permute-start(bf16[96,4096]{1,0:T(8,128)(2,1)} %get-tuple-element.28.stacked), channel_id=1, source_target_pairs={{1,2},{2,1},{3,4},{4,3},{5,6},{6,5},{7,8},{8,7},{9,10},{10,9},{11,... | collective-permute-start | bytes 2359304 | tf_op jit(solution)/shard_map/ppermute | solution.py:446
  8.3 4.3 %collective-permute-start = (bf16[96,4096]{1,0:T(8,128)(2,1)}, bf16[96,4096]{1,0:T(8,128)(2,1)S(1)}, u32[]{:S(2)}, u32[]{:S(2)}) collective-permute-start(bf16[96,4096]{1,0:T(8,128)(2,1)} %get-tuple-element.28.stacked), channel_id=1, source_target_pairs={{0,1},{1,0},{2,3},{3,2},{4,5},{5,4},{6,7},{7,6},{8,9},{9,8},{10,11... | collective-permute-start | bytes 2359304 | tf_op jit(solution)/shard_map/ppermute | solution.py:445
  12.6 0.0 copy-done.2
  12.6 1.1 %copy-done.1 = bf16[96,4096]{1,0:T(8,128)(2,1)S(1)} copy-done((bf16[96,4096]{1,0:T(8,128)(2,1)S(1)}, bf16[96,4096]{1,0:T(8,128)(2,1)}, u32[]{:S(2)}) %copy-start.1) | copy-done | bytes 786456
  13.8 4.4 %shard_map.87 = (bf16[30,144,256]{2,1,0:T(8,128)(2,1)S(1)}, bf16[30,256,144]{2,1,0:T(8,128)(2,1)S(1)}, bf16[30,32,256]{2,1,0:T(8,128)(2,1)S(1)}, bf16[15,256,512...) custom-call(bf16[96,4096]{1,0:T(8,128)(2,1)S(1)} %copy-done.1, s32[15,256]{1,0:T(8,128)S(1)} %copy-done.2), custom_call_target="tpu_custom_call" | custom-call | flops 10000000000 | bytes 1048576 | tf_op jit(solution)/shard_map/pallas_call | solution.py:450
  18.2 0.1 collective-permute-start.2
  18.3 0.0 copy-done.4
  18.3 0.0 copy-start
  18.3 6.4 %shard_map.88._.rest_0_ = f32[30,32,256]{2,1,0:T(8,128)S(1)} custom-call(s32[13,128]{1,0:T(8,128)S(1)} %copy-done.4, bf16[30,144,256]{2,1,0:T(8,128)(2,1)S(1)} %get-tuple-element.29.src.own_src, bf16[30,256,144]{2,1,0:T(8,128)(2,1)S(1)} %get-tuple-element.30.tgt, bf16[30,32,256]{2,1,0:T(8,128)(2,1)S(1)} %get-tuple-element.31.wts.own_wts, ...), custom_call_target="tpu_custom_call" | custom-call | flops 10000000000 | bytes 1048576 | tf_op jit(solution)/shard_map/pallas_call | solution.py:470
  24.7 0.0 collective-permute-done.2.sibling.rest_0_
  24.8 0.7 %shard_map.89 = (bf16[112,256]{1,0:T(8,128)(2,1)S(1)}, bf16[256,144]{1,0:T(8,128)(2,1)S(1)}, bf16[256,256]{1,0:T(8,128)(2,1)S(1)}) custom-call(s32[1]{0:T(128)} %bitcast.place, bf16[112,256]{1,0:T(8,128)(2,1)S(1)} %get-tuple-element.32._.own, bf16[112,256]{1,0:T(8,128)(2,1)S(1)} %collective-permute-done.2.sibling.rest_0_, s32[30,256]{1,0:T(8,128)S(1)} %copy-done, ...), custom_call_target="tpu_custom_call" | custom-call | flops 100000000 | bytes 1048576 | tf_op jit(solution)/shard_map/pallas_call | solution.py:525
  25.5 1.6 %collective-permute-start.3 = (bf16[112,256]{1,0:T(8,128)(2,1)S(1)}, bf16[112,256]{1,0:T(8,128)(2,1)S(1)}, u32[]{:S(2)}, u32[]{:S(2)}) collective-permute-start(bf16[112,256]{1,0:T(8,128)(2,1)S(1)} %get-tuple-element.33._.own), channel_id=1, source_target_pairs={{0,2},{1,3},{2,0},{3,1},{4,6},{5,7},{6,4},{7,5},{8,10},{9,11},{10,... | collective-permute-start | bytes 172040 | tf_op jit(solution)/shard_map/ppermute | solution.py:507
  27.0 6.5 %shard_map.90._._acc = f32[30,32,256]{2,1,0:T(8,128)S(1)} custom-call(s32[13,128]{1,0:T(8,128)S(1)} %copy-done.4, bf16[30,144,256]{2,1,0:T(8,128)(2,1)S(1)} %get-tuple-element.29.src.own_src, bf16[30,256,144]{2,1,0:T(8,128)(2,1)S(1)} %get-tuple-element.30.tgt, ...), custom_call_target="tpu_custom_call", output_to_operand_aliasing={{}: (5, {})} | custom-call | flops 10000000000 | bytes 1048576 | tf_op jit(solution)/shard_map/pallas_call | solution.py:470
  33.6 0.0 collective-permute-done.3.sibling.rest_1_
  33.6 0.7 %shard_map.91 = (bf16[112,256]{1,0:T(8,128)(2,1)S(1)}, bf16[256,144]{1,0:T(8,128)(2,1)S(1)}, bf16[256,256]{1,0:T(8,128)(2,1)S(1)}) custom-call(s32[1]{0:T(128)} %bitcast.place, bf16[112,256]{1,0:T(8,128)(2,1)S(1)} %get-tuple-element.33._.own, bf16[112,256]{1,0:T(8,128)(2,1)S(1)} %collective-permute-done.3.sibling.rest_1_, s32[30,256]{1,0:T(8,128)S(1)} %copy-done, ...), custom_call_target="tpu_custom_call" | custom-call | flops 100000000 | bytes 1048576 | tf_op jit(solution)/shard_map/pallas_call | solution.py:525
  34.3 1.6 %collective-permute-start.4 = (bf16[112,256]{1,0:T(8,128)(2,1)S(1)}, bf16[112,256]{1,0:T(8,128)(2,1)S(1)}, u32[]{:S(2)}, u32[]{:S(2)}) collective-permute-start(bf16[112,256]{1,0:T(8,128)(2,1)S(1)} %get-tuple-element.34._.own), channel_id=1, source_target_pairs={{0,4},{1,5},{2,6},{3,7},{4,0},{5,1},{6,2},{7,3},{8,12},{9,13},{10,... | collective-permute-start | bytes 172040 | tf_op jit(solution)/shard_map/ppermute | solution.py:507
  35.9 0.0 collective-permute-done.1.across
  35.9 0.0 collective-permute-done.within
  35.9 3.5 %shard_map.92 = (f32[30,32,256]{2,1,0:T(8,128)S(1)}, bf16[48,144,256]{2,1,0:T(8,128)(2,1)S(1)}, bf16[48,32,256]{2,1,0:T(8,128)(2,1)S(1)}) custom-call(s32[13,128]{1,0:T(8,128)S(1)} %copy-done.4, s32[1]{0:T(128)} %bitcast.place, bf16[96,4096]{1,0:T(8,128)(2,1)S(1)} %collective-permute-done.within, ...), custom_call_target="tpu_custom_call", output_to_operand_aliasing={{0}: (8, {})} | custom-call | flops 10000000000 | bytes 1048576 | tf_op jit(solution)/shard_map/pallas_call | solution.py:480
  39.4 0.0 collective-permute-done.4.sibling.rest_2_
  39.4 0.7 %shard_map.93 = (bf16[112,256]{1,0:T(8,128)(2,1)S(1)}, bf16[256,144]{1,0:T(8,128)(2,1)S(1)}, bf16[256,256]{1,0:T(8,128)(2,1)S(1)}) custom-call(s32[1]{0:T(128)} %bitcast.place, bf16[112,256]{1,0:T(8,128)(2,1)S(1)} %get-tuple-element.34._.own, bf16[112,256]{1,0:T(8,128)(2,1)S(1)} %collective-permute-done.4.sibling.rest_2_, s32[30,256]{1,0:T(8,128)S(1)} %copy-done, ...), custom_call_target="tpu_custom_call" | custom-call | flops 100000000 | bytes 1048576 | tf_op jit(solution)/shard_map/pallas_call | solution.py:525
  40.1 1.6 %collective-permute-start.5 = (bf16[112,256]{1,0:T(8,128)(2,1)S(1)}, bf16[112,256]{1,0:T(8,128)(2,1)S(1)}, u32[]{:S(2)}, u32[]{:S(2)}) collective-permute-start(bf16[112,256]{1,0:T(8,128)(2,1)S(1)} %get-tuple-element.38._.own), channel_id=1, source_target_pairs={{0,8},{1,9},{2,10},{3,11},{4,12},{5,13},{6,14},{7,15},{8,0},{9,1},... | collective-permute-start | bytes 172040 | tf_op jit(solution)/shard_map/ppermute | solution.py:507
  41.7 3.2 %shard_map.94._._acc = f32[30,32,256]{2,1,0:T(8,128)S(1)} custom-call(s32[13,128]{1,0:T(8,128)S(1)} %copy-done.4, bf16[48,144,256]{2,1,0:T(8,128)(2,1)S(1)} %get-tuple-element.35.src, bf16[30,256,144]{2,1,0:T(8,128)(2,1)S(1)} %get-tuple-element.30.tgt, bf16[48,32,256]{2,1,0:T(8,128)(2,1)S(1)} %get-tuple-element.36.wts, ...), custom_call_target="tpu_custom_call", output_to_operand_aliasing={{}: (5, {})} | custom-call | flops 10000000000 | bytes 1048576 | tf_op jit(solution)/shard_map/pallas_call | solution.py:494
  44.9 0.0 collective-permute-done.5.sibling.rest_3_
  44.9 0.7 %shard_map.95 = (bf16[112,256]{1,0:T(8,128)(2,1)S(1)}, bf16[256,144]{1,0:T(8,128)(2,1)S(1)}, bf16[256,256]{1,0:T(8,128)(2,1)S(1)}) custom-call(s32[1]{0:T(128)} %bitcast.place, bf16[112,256]{1,0:T(8,128)(2,1)S(1)} %get-tuple-element.38._.own, bf16[112,256]{1,0:T(8,128)(2,1)S(1)} %collective-permute-done.5.sibling.rest_3_, s32[30,256]{1,0:T(8,128)S(1)} %copy-done, ...), custom_call_target="tpu_custom_call" | custom-call | flops 100000000 | bytes 1048576 | tf_op jit(solution)/shard_map/pallas_call | solution.py:525
  45.6 0.0 copy-start.3
  45.6 2.1 %collective-permute-start.6 = (bf16[112,256]{1,0:T(8,128)(2,1)S(1)}, bf16[112,256]{1,0:T(8,128)(2,1)S(1)}, u32[]{:S(2)}, u32[]{:S(2)}) collective-permute-start(bf16[112,256]{1,0:T(8,128)(2,1)S(1)} %get-tuple-element.39._), channel_id=1, source_target_pairs={{0,16},{1,17},{2,18},{3,19},{4,20},{5,21},{6,22},{7,23},{8,24},{9,... | collective-permute-start | bytes 172040 | tf_op jit(solution)/shard_map/ppermute | solution.py:507
  47.7 3.2 %shard_map.96.all_acc = f32[30,32,256]{2,1,0:T(8,128)S(1)} custom-call(s32[13,128]{1,0:T(8,128)S(1)} %copy-done.4, bf16[48,144,256]{2,1,0:T(8,128)(2,1)S(1)} %get-tuple-element.35.src, bf16[30,256,144]{2,1,0:T(8,128)(2,1)S(1)} %get-tuple-element.30.tgt, bf16[48,32,256]{2,1,0:T(8,128)(2,1)S(1)} %get-tuple-element.36.wts, ...), custom_call_target="tpu_custom_call", output_to_operand_aliasing={{}: (5, {})} | custom-call | flops 10000000000 | bytes 1048576 | tf_op jit(solution)/shard_map/pallas_call | solution.py:494
  50.9 0.5 collective-permute-done.6.rest_4_
  51.4 8.0 %shard_map.97 = (f32[32,4096]{1,0:T(8,128)}, f32[32,256]{1,0:T(8,128)}) custom-call(s32[13,128]{1,0:T(8,128)S(1)} %copy-done.4, bf16[48,144,256]{2,1,0:T(8,128)(2,1)S(1)} %get-tuple-element.35.src, bf16[30,256,144]{2,1,0:T(8,128)(2,1)S(1)} %get-tuple-element.30.tgt, bf16[48,32,256]{2,1,0:T(8,128)(2,1)S(1)} %get-tuple-element.36.wts, ...), custom_call_target="tpu_custom_call" | custom-call | flops 10000000000 | bytes 1048576 | tf_op jit(solution)/shard_map/pallas_call | solution.py:542
  (4 shorter events, 0.0 us)
Async XLA Ops:
  0.6 12.0 %copy-start.2 = (s32[15,256]{1,0:T(8,128)S(1)}, s32[15,256]{1,0:T(8,128)}, u32[]{:S(2)}) copy-start(s32[15,256]{1,0:T(8,128)} %skel.5) | copy-start | bytes 46084
  7.4 28.5 %collective-permute-start.1 = (bf16[96,4096]{1,0:T(8,128)(2,1)}, bf16[96,4096]{1,0:T(8,128)(2,1)S(1)}, u32[]{:S(2)}, u32[]{:S(2)}) collective-permute-start(bf16[96,4096]{1,0:T(8,128)(2,1)} %get-tuple-element.28.stacked), channel_id=1, source_target_pairs={{1,2},{2,1},{3,4},{4,3},{5,6},{6,5},{7,8},{8,7},{9,10},{10,9},{11,... | collective-permute-start | bytes 2359304 | tf_op jit(solution)/shard_map/ppermute | solution.py:446
  8.3 27.6 %collective-permute-start = (bf16[96,4096]{1,0:T(8,128)(2,1)}, bf16[96,4096]{1,0:T(8,128)(2,1)S(1)}, u32[]{:S(2)}, u32[]{:S(2)}) collective-permute-start(bf16[96,4096]{1,0:T(8,128)(2,1)} %get-tuple-element.28.stacked), channel_id=1, source_target_pairs={{0,1},{1,0},{2,3},{3,2},{4,5},{5,4},{6,7},{7,6},{8,9},{9,8},{10,11... | collective-permute-start | bytes 2359304 | tf_op jit(solution)/shard_map/ppermute | solution.py:445
  12.6 1.1 %copy-start.1 = (bf16[96,4096]{1,0:T(8,128)(2,1)S(1)}, bf16[96,4096]{1,0:T(8,128)(2,1)}, u32[]{:S(2)}) copy-start(bf16[96,4096]{1,0:T(8,128)(2,1)} %get-tuple-element.28.stacked) | copy-start | bytes 2359300
  13.8 4.5 %copy-start.4 = (s32[13,128]{1,0:T(8,128)S(1)}, s32[13,128]{1,0:T(8,128)}, u32[]{:S(2)}) copy-start(s32[13,128]{1,0:T(8,128)} %get-tuple-element.27.pairs) | copy-start | bytes 19972
  18.2 6.5 %collective-permute-start.2 = (bf16[112,256]{1,0:T(8,128)(2,1)S(1)}, bf16[112,256]{1,0:T(8,128)(2,1)S(1)}, u32[]{:S(2)}, u32[]{:S(2)}) collective-permute-start(bf16[112,256]{1,0:T(8,128)(2,1)S(1)} %get-tuple-element.32._.own), channel_id=1, source_target_pairs={{0,1},{1,0},{2,3},{3,2},{4,5},{5,4},{6,7},{7,6},{8,9},{9,8},{10,11... | collective-permute-start | bytes 172040 | tf_op jit(solution)/shard_map/ppermute | solution.py:507
  18.3 6.5 %copy-start = (s32[30,256]{1,0:T(8,128)S(1)}, s32[30,256]{1,0:T(8,128)}, u32[]{:S(2)}) copy-start(s32[30,256]{1,0:T(8,128)} %skel.9) | copy-start | bytes 92164
  25.5 8.1 %collective-permute-start.3 = (bf16[112,256]{1,0:T(8,128)(2,1)S(1)}, bf16[112,256]{1,0:T(8,128)(2,1)S(1)}, u32[]{:S(2)}, u32[]{:S(2)}) collective-permute-start(bf16[112,256]{1,0:T(8,128)(2,1)S(1)} %get-tuple-element.33._.own), channel_id=1, source_target_pairs={{0,2},{1,3},{2,0},{3,1},{4,6},{5,7},{6,4},{7,5},{8,10},{9,11},{10,... | collective-permute-start | bytes 172040 | tf_op jit(solution)/shard_map/ppermute | solution.py:507
  34.3 5.1 %collective-permute-start.4 = (bf16[112,256]{1,0:T(8,128)(2,1)S(1)}, bf16[112,256]{1,0:T(8,128)(2,1)S(1)}, u32[]{:S(2)}, u32[]{:S(2)}) collective-permute-start(bf16[112,256]{1,0:T(8,128)(2,1)S(1)} %get-tuple-element.34._.own), channel_id=1, source_target_pairs={{0,4},{1,5},{2,6},{3,7},{4,0},{5,1},{6,2},{7,3},{8,12},{9,13},{10,... | collective-permute-start | bytes 172040 | tf_op jit(solution)/shard_map/ppermute | solution.py:507
  40.1 4.8 %collective-permute-start.5 = (bf16[112,256]{1,0:T(8,128)(2,1)S(1)}, bf16[112,256]{1,0:T(8,128)(2,1)S(1)}, u32[]{:S(2)}, u32[]{:S(2)}) collective-permute-start(bf16[112,256]{1,0:T(8,128)(2,1)S(1)} %get-tuple-element.38._.own), channel_id=1, source_target_pairs={{0,8},{1,9},{2,10},{3,11},{4,12},{5,13},{6,14},{7,15},{8,0},{9,1},... | collective-permute-start | bytes 172040 | tf_op jit(solution)/shard_map/ppermute | solution.py:507
  45.6 5.8 %copy-start.3 = (s32[1,4096]{1,0:T(1,128)S(1)}, s32[1,4096]{1,0:T(1,128)}, u32[]{:S(2)}) copy-start(s32[1,4096]{1,0:T(1,128)} %order.3) | copy-start | bytes 49156
  45.6 5.8 %collective-permute-start.6 = (bf16[112,256]{1,0:T(8,128)(2,1)S(1)}, bf16[112,256]{1,0:T(8,128)(2,1)S(1)}, u32[]{:S(2)}, u32[]{:S(2)}) collective-permute-start(bf16[112,256]{1,0:T(8,128)(2,1)S(1)} %get-tuple-element.39._), channel_id=1, source_target_pairs={{0,16},{1,17},{2,18},{3,19},{4,20},{5,21},{6,22},{7,23},{8,24},{9,... | collective-permute-start | bytes 172040 | tf_op jit(solution)/shard_map/ppermute | solution.py:507
